TPU v7x, 32 devices: a whole 2x2x4 slice. The times are simulated.
32 devices in a mesh: blk: 16 (over z, y, x), mc: 2 (over core).
Axes of the slice: x: 2, y: 2, z: 4, core: 2. Of those that a mesh axis runs over, the one named last changes fastest.
Arguments:
- batch_ids: int32 [512], P('blk'), may hold values from 0 to 4095, as said below
- cond_ids: int32 [512, 3], P('blk'), may hold values from 0 to 4095, as said below
- home: int32 [4096], replicated, may hold values from 0 to 4095, as said below
- latent: bfloat16 [4096, 32, 256], P('blk', 'mc'), may hold values from -6 to 6
- diag_factor: bfloat16 [512, 256, 256], P('blk'), may hold values from -0.375 to 0.375
- cond_factor: bfloat16 [512, 3, 256, 256], P('blk'), may hold values from -0.375 to 0.375
- obs: float32 [512, 256], P('blk'), may hold values from -6 to 6
- noise_prec: float32 [], replicated, may hold values from 0.5 to 2
Outputs:
- mean_grad: float32 [4096, 256], P('blk', 'mc')
Inputs may be any that keep to these rules, and one draw needn't show every extreme that they name: home is a permutation; block b is stored at position home[b], on index home[b] // 256 of blk. `batch_ids`: of the 128 blocks named by one index's rows (each row's own block and its conditioning blocks, repeats counted), at most 20 are stored on any one index of blk. `cond_ids`: counted together with batch_ids as stated there.
All inputs are finite; a program needn't handle non-finite values.
Results may differ from a plain program's by a relative error of at most 0.0029.
Values may be sent and summed in bfloat16 or wider, within the bound.
A program may use at most 64 MiB of HBM per device.

v0:
```python
import jax
import jax.numpy as jnp
from jax import lax
from jax.sharding import PartitionSpec as P

freedom = 4.0


def body(batch_ids, cond_ids, home, latent, diag_factor, cond_factor, obs, noise_prec):
    owners = lax.axis_size("blk")
    per_owner = latent.shape[0]
    draw_count = latent.shape[1]
    block_width = latent.shape[2]
    row_count = batch_ids.shape[0]
    want_count = 4 * row_count
    capacity = max(2, 10 * row_count // owners)
    inverse_draws = 1.0 / (draw_count * lax.axis_size("mc"))
    block_ids = jnp.concatenate([batch_ids[:, None], cond_ids], axis=1).reshape(-1)
    wanted = home[block_ids]
    dest_dev = wanted // per_owner
    slot_idx = wanted % per_owner
    earlier = jnp.arange(want_count)[:, None] > jnp.arange(want_count)[None, :]
    same_dest = dest_dev[:, None] == dest_dev[None, :]
    rank_idx = jnp.sum(same_dest & earlier, axis=1)
    send_spot = dest_dev * capacity + rank_idx
    outbox = (
        jnp.full((owners * capacity,), -1, jnp.int32)
        .at[send_spot]
        .set(slot_idx)
        .reshape(owners, capacity)
    )
    in_slots = lax.all_to_all(outbox, "blk", split_axis=0, concat_axis=0, tiled=True)
    is_valid = in_slots >= 0
    outgoing = latent[jnp.maximum(in_slots, 0)]
    fetched = lax.all_to_all(outgoing, "blk", split_axis=0, concat_axis=0, tiled=True)
    picked = fetched.reshape(owners * capacity, draw_count, block_width)[send_spot]
    picked = picked.reshape(row_count, 4, draw_count, block_width)
    own_panel = picked[:, 0]
    near_panel = picked[:, 1:]
    lower_mask = jnp.arange(block_width)[:, None] >= jnp.arange(block_width)[None, :]
    lower_diag = jnp.where(lower_mask[None, :, :], diag_factor, jnp.zeros_like(diag_factor))
    whitened = jnp.einsum("rsj,rij->rsi", own_panel, lower_diag, preferred_element_type=jnp.float32)
    whitened = whitened + jnp.einsum(
        "rksj,rkij->rsi", near_panel, cond_factor, preferred_element_type=jnp.float32
    )
    scored = (freedom + 1.0) * whitened / (freedom + whitened * whitened)
    white_low = scored.astype(jnp.bfloat16)
    back_diag = jnp.einsum("rsi,rij->rj", white_low, lower_diag, preferred_element_type=jnp.float32)
    likely = noise_prec * jnp.sum(obs[:, None, :] - own_panel.astype(jnp.float32), axis=1)
    self_term = (likely - back_diag) * inverse_draws
    cond_term = (
        -jnp.einsum("rsi,rkij->rkj", white_low, cond_factor, preferred_element_type=jnp.float32)
        * inverse_draws
    )
    grad_terms = jnp.concatenate([self_term[:, None, :], cond_term], axis=1).reshape(
        want_count, block_width
    )
    target_slot = jnp.where(is_valid, in_slots, per_owner).reshape(-1)
    outbox_terms = (
        jnp.zeros((owners * capacity, block_width), jnp.float32).at[send_spot].set(grad_terms)
    )
    inbox_terms = lax.all_to_all(
        outbox_terms.reshape(owners, capacity, block_width),
        "blk",
        split_axis=0,
        concat_axis=0,
        tiled=True,
    )
    stored = (
        jnp.zeros((per_owner, block_width), jnp.float32)
        .at[target_slot]
        .add(inbox_terms.reshape(-1, block_width), mode="drop")
    )
    return lax.psum_scatter(stored, "mc", scatter_dimension=1, tiled=True)


def solution(mesh):
    placed = (
        P("blk"),
        P("blk", None),
        P(),
        P("blk", "mc", None),
        P("blk", None, None),
        P("blk", None, None, None),
        P("blk", None),
        P(),
    )
    return jax.shard_map(
        body, mesh=mesh, in_specs=placed, out_specs=P("blk", "mc"), check_vma=False
    )
```

profile of v0, /device:TPU:0, one launch (start us, length us, event | category | flops | bytes accessed | tf_op | source)
XLA Modules:
  0.0 147.1 jit_solution(8593083091177291464)
XLA Ops:
  6.5 0.8 pad_add_fusion
  7.4 0.1 copy.13
  7.5 0.1 reshape.192
  7.6 1.6 %gather_fusion = s32[128]{0:T(128)S(1)} fusion(s32[4096]{0:T(1024)} %param.10, s32[1024]{0:T(1024)S(1)} %pad_clamp_fusion.2), kind=kCustom, calls=%fused_computation | custom fusion | bytes 1536 | tf_op jit(solution)/shard_map/gather | solution.py:19
  9.3 0.2 convert_reduce_fusion.1
  9.5 1.0 scatter_custom_fusion
  10.4 0.1 all_to_all.14
  10.5 15.4 %all_to_all.22 = s32[16,1,20]{2,1,0:T(1,128)S(1)} all-to-all(s32[16,1,20]{2,1,0:T(1,128)S(1)} %all_to_all.14), channel_id=1, replica_groups=mesh['blk'=16,'mc'=2] {'blk'}, dimensions={0} | all-to-all | bytes 2560 | tf_op jit(solution)/shard_map/all_to_all | solution.py:32
  25.9 0.5 broadcast.231
  26.4 0.7 maximum_reduce_fusion
  27.1 0.1 reshape.208
  27.3 3.0 %gather_fusion.1 = bf16[320,16,256]{2,1,0:T(8,128)(2,1)} fusion(bf16[256,16,256]{2,1,0:T(8,128)(2,1)S(1)} %copy-done, s32[1024]{0:T(1024)S(1)} %pad_clamp_fusion.1), kind=kCustom, calls=%fused_computation.1 | custom fusion | bytes 5244160 | tf_op jit(solution)/shard_map/gather | solution.py:34
  30.3 4.4 %all-to-all-start.1 = ((bf16[16,20,16,256]{3,2,1,0:T(8,128)(2,1)}), bf16[16,20,16,256]{3,2,1,0:T(8,128)(2,1)}, u32[]{:S(2)}, u32[]{:S(2)}) async-start(bf16[16,20,16,256]{3,2,1,0:T(8,128)(2,1)} %bitcast.53), calls=%async_computation.1 | async-start | bytes 5242880 | tf_op jit(solution)/shard_map/all_to_all | solution.py:35
  35.4 50.5 %all-to-all-done.1 = bf16[16,20,16,256]{3,2,1,0:T(8,128)(2,1)} async-done(((bf16[16,20,16,256]{3,2,1,0:T(8,128)(2,1)}), bf16[16,20,16,256]{3,2,1,0:T(8,128)(2,1)}, u32[]{:S(2)}, u32[]{:S(2)}) %all-to-all-start.1) | async-done | bytes 2621472 | tf_op jit(solution)/shard_map/all_to_all | solution.py:35
  85.9 2.4 %gather_fusion.2 = bf16[128,16,256]{2,1,0:T(8,128)(2,1)S(1)} fusion(bf16[320,16,256]{2,1,0:T(8,128)(2,1)} %bitcast.6, s32[1024]{0:T(1024)S(1)} %pad_clamp_fusion), kind=kCustom, calls=%fused_computation.2 | custom fusion | bytes 2097664 | tf_op jit(solution)/shard_map/gather | solution.py:36
  88.3 0.0 slice-start
  88.3 4.3 %fusion.1 = f32[32,16,256]{2,1,0:T(8,128)} fusion(bf16[32,256,256]{2,1,0:T(8,128)(2,1)} %param.12, pred[256,256]{1,0:T(8,128)(4,1)S(1)} %iota_compare_fusion, bf16[32,4,16,256]{3,2,1,0:T(8,128)(2,1)S(1)} %bitcast.54), kind=kOutput, calls=%fused_computation.8 | convolution fusion | flops 69206016 | bytes 5046272 | tf_op jit(solution)/shard_map/rsj,rij->rsi/dot_general | solution.py:42
  92.7 8.2 %convert_reduce_fusion = bf16[32,256]{1,0:T(8,128)(2,1)S(1)} fusion(f32[32,16,256]{2,1,0:T(8,128)} %fusion.1, bf16[32,4,16,256]{3,2,1,0:T(8,128)(2,1)S(1)} %bitcast.55, bf16[32,3,256,256]{3,2,1,0:T(8,128)(2,1)} %param.13), kind=kOutput, calls=%fused_computation.13 | convolution fusion | flops 202366976 | bytes 14172160 | tf_op jit(solution)/shard_map/rksj,rkij->rsi/dot_general | solution.py:43
  100.9 0.0 copy-start.1
  100.9 2.9 %fusion = f32[32,1,256]{2,1,0:T(1,128)S(1)} fusion(bf16[32,256,256]{2,1,0:T(8,128)(2,1)} %param.12, pred[256,256]{1,0:T(8,128)(4,1)S(1)} %iota_compare_fusion, bf16[32,256,1]{1,0,2:T(8,128)(2,1)S(1)} %bitcast.57), kind=kOutput, calls=%fused_computation.7 | convolution fusion | flops 6291456 | bytes 4308992 | tf_op jit(solution)/shard_map/rsi,rij->rj/dot_general | solution.py:48
  103.7 0.1 subtract_reduce_fusion
  104.0 1.7 %fusion.12 = f32[32,1,3,256]{3,1,2,0:T(1,128)S(1)} fusion(bf16[32,3,256,256]{3,2,1,0:T(8,128)(2,1)S(1)} %bitcast.52, bf16[32,256,1,1]{1,0,2,3:T(8,128)(2,1)S(1)} %bitcast.58), kind=kOutput, calls=%fused_computation.30 | convolution fusion | flops 12582912 | bytes 12697600 | tf_op jit(solution)/shard_map/rsi,rkij->rkj/dot_general | solution.py:52
  105.7 0.1 pad_maximum_fusion
  105.9 1.1 scatter_custom_fusion.1
  107.0 0.8 reshape.196
  107.7 11.9 %all-to-all-start.2 = ((f32[16,20,256]{2,1,0:T(8,128)}), f32[16,20,256]{2,1,0:T(8,128)S(1)}, u32[]{:S(2)}, u32[]{:S(2)}) async-start(f32[16,20,256]{2,1,0:T(8,128)} %reshape.196), calls=%async_computation.2 | async-start | bytes 786432 | tf_op jit(solution)/shard_map/all_to_all | solution.py:62
  119.6 0.0 reduce-scatter.2.cloned.1.call-start
  119.7 0.1 all_to_all.16
  119.8 11.6 %all-to-all-done.2 = f32[16,20,256]{2,1,0:T(8,128)S(1)} async-done(((f32[16,20,256]{2,1,0:T(8,128)}), f32[16,20,256]{2,1,0:T(8,128)S(1)}, u32[]{:S(2)}, u32[]{:S(2)}) %all-to-all-start.2) | async-done | bytes 327712 | tf_op jit(solution)/shard_map/all_to_all | solution.py:62
  131.5 2.9 %scatter_custom_fusion.2 = f32[256,256]{1,0:T(8,128)} fusion(s32[320]{0:T(512)S(1)} %fusion.15, f32[320,256]{1,0:T(8,128)S(1)} %reshape.242, f32[]{:T(128)} %constant.17.clone.1), kind=kCustom, calls=%fused_computation.23 | custom fusion | flops 81920 | bytes 262148 | tf_op jit(solution)/shard_map/scatter-add | solution.py:72
  134.4 0.0 reduce-scatter.2.cloned.1.call-update
  134.4 5.8 %reduce-scatter.2.cloned.1.call-done = f32[256,128]{1,0:T(8,128)} async-done(((f32[256,256]{1,0:T(8,128)}), f32[256,128]{1,0:T(8,128)}) %reduce-scatter.2.cloned.1.call-update) | async-done | bytes 131088 | tf_op jit(solution)/shard_map/reduce_scatter | solution.py:74
  (22 shorter events, 0.3 us)
Async XLA Ops:
  6.5 20.7 %copy-start = (bf16[256,16,256]{2,1,0:T(8,128)(2,1)S(1)}, bf16[256,16,256]{2,1,0:T(8,128)(2,1)}, u32[]{:S(2)}) copy-start(bf16[256,16,256]{2,1,0:T(8,128)(2,1)} %param.11) | copy-start | bytes 6291460
  30.3 55.6 %all-to-all-start.1 = ((bf16[16,20,16,256]{3,2,1,0:T(8,128)(2,1)}), bf16[16,20,16,256]{3,2,1,0:T(8,128)(2,1)}, u32[]{:S(2)}, u32[]{:S(2)}) async-start(bf16[16,20,16,256]{3,2,1,0:T(8,128)(2,1)} %bitcast.53), calls=%async_computation.1 | async-start | bytes 5242880 | tf_op jit(solution)/shard_map/all_to_all | solution.py:35
  88.3 15.6 %slice-start = ((s8[12582912]{0:T(1024)(128)(4,1)}), s8[4194304]{0:T(1024)(128)(4,1)S(1)}, s32[]{:S(2)}) async-start(s8[12582912]{0:T(1024)(128)(4,1)} %bitcast.51), calls=%async_computation.5 | async-start | bytes 8388608
  92.7 11.3 %slice-start.1 = ((s8[12582912]{0:T(1024)(128)(4,1)}), s8[4194304]{0:T(1024)(128)(4,1)S(1)}, s32[]{:S(2)}) async-start(s8[12582912]{0:T(1024)(128)(4,1)} %bitcast.51), calls=%async_computation.6 | async-start | bytes 8388608
  92.7 11.3 %slice-start.2 = ((s8[12582912]{0:T(1024)(128)(4,1)}), s8[4194304]{0:T(1024)(128)(4,1)S(1)}, s32[]{:S(2)}) async-start(s8[12582912]{0:T(1024)(128)(4,1)} %bitcast.51), calls=%async_computation.7 | async-start | bytes 8388608
  100.9 2.9 %copy-start.1 = (f32[32,256]{1,0:T(8,128)S(1)}, f32[32,256]{1,0:T(8,128)}, u32[]{:S(2)}) copy-start(f32[32,256]{1,0:T(8,128)} %param.14) | copy-start | bytes 98308
  107.7 23.7 %all-to-all-start.2 = ((f32[16,20,256]{2,1,0:T(8,128)}), f32[16,20,256]{2,1,0:T(8,128)S(1)}, u32[]{:S(2)}, u32[]{:S(2)}) async-start(f32[16,20,256]{2,1,0:T(8,128)} %reshape.196), calls=%async_computation.2 | async-start | bytes 786432 | tf_op jit(solution)/shard_map/all_to_all | solution.py:62
  119.6 20.6 %reduce-scatter.2.cloned.1.call-start = ((), (), s32[]{:S(2)}) async-start(), calls=%async_computation.4 | async-start | bytes 393216 | tf_op jit(solution)/shard_map/reduce_scatter | solution.py:74
Sparse Core Ops, SparseCore 0:
  134.5 5.6 reduce-scatter.1
where the time goes:
time: 148 us; the launch traced here: 147 us
  waiting for transfers between devices  68 us (46%)
  matrix products  17.1 us (12%)
  starting transfers between devices  16.4 us (11%)
  blocking collectives  15.4 us (10%)
  between operations  14.3 us (10%)
  local copies, waits for them, and re-layouts  11 us (7%)
  other arithmetic  5 us (3%)
    all_to_all x1, waiting for transfers between devices, body(): lax.all_to_all(outgoing, 'blk', split_axis=0, concat_axis=0, tiled=True)  50.5 us
    all_to_all x1, blocking collectives, body(): lax.all_to_all(outbox, 'blk', split_axis=0, concat_axis=0, tiled=True)  15.4 us
    all_to_all x1, starting transfers between devices, body(): lax.all_to_all(outbox_terms.reshape(owners, capacity, block_width), 'blk'...  11.9 us
    all_to_all x1, waiting for transfers between devices, body(): lax.all_to_all(outbox_terms.reshape(owners, capacity, block_width), 'blk'...  11.6 us
    dot_general x1, matrix products, body(): jnp.einsum('rksj,rkij->rsi', near_panel, cond_factor, preferred_element_t...  8.18 us
    reduce_scatter x1, waiting for transfers between devices, body(): return lax.psum_scatter(stored, 'mc', scatter_dimension=1, tiled=True)  5.85 us
    all_to_all x1, starting transfers between devices, body(): lax.all_to_all(outgoing, 'blk', split_axis=0, concat_axis=0, tiled=True)  4.45 us
    dot_general x1, matrix products, body(): jnp.einsum('rsj,rij->rsi', own_panel, lower_diag, preferred_element_type=...  4.34 us
  transfers between devices with their start and end apart: 3, of which 3 were waited for; matrix products, arithmetic and copies ran while one was open for 0% of the time, Pallas kernels for 0%

commit v1 on v0

v1 whole, which is shorter than its diff:
```python
import functools

import jax
import jax.numpy as jnp
from jax import lax
from jax.experimental import pallas as pl
from jax.experimental.pallas import tpu as pltpu
from jax.sharding import PartitionSpec as P

freedom = 4.0
MESH = pl.DeviceIdType.MESH
f32 = jnp.float32
bf16 = jnp.bfloat16
NT = (((1,), (1,)), ((), ()))


def kernel(
    n,
    cap,
    in_slots,
    pick,
    inverse,
    target,
    noise,
    latent,
    diag,
    cond,
    obs,
    out,
    outgoing,
    fetched,
    lower,
    near,
    sums,
    sums_in,
    terms,
    outbox,
    inbox,
    load_sem,
    lat_send,
    lat_recv,
    pair_sem,
    term_send,
    term_recv,
):
    rows = obs.shape[0]
    draws = latent.shape[1]
    width = latent.shape[2]
    half = width // 2
    pad = outbox.shape[1]
    me = lax.axis_index("blk")
    core = lax.axis_index("mc")
    partner = (me, 1 - core)
    inverse_draws = 1.0 / (2 * draws)

    load_diag = pltpu.make_async_copy(diag, lower, load_sem.at[0])
    load_cond = pltpu.make_async_copy(cond, near, load_sem.at[1])
    load_diag.start()
    load_cond.start()

    barrier = pltpu.get_barrier_semaphore()

    @pl.loop(1, n)
    def _(o):
        pl.semaphore_signal(
            barrier, inc=1, device_id=(lax.rem(me + o, n), core), device_id_type=MESH
        )

    pl.semaphore_signal(barrier, inc=1, device_id=partner, device_id_type=MESH)
    pl.semaphore_wait(barrier, n)

    def latent_copy(o):
        dst = lax.rem(me + o, n)
        return pltpu.make_async_remote_copy(
            src_ref=outgoing.at[dst],
            dst_ref=fetched.at[pl.ds(me * cap, cap)],
            send_sem=lat_send.at[o],
            recv_sem=lat_recv.at[o],
            device_id=(dst, core),
            device_id_type=MESH,
        )

    @pl.loop(1, n)
    def _(o):
        dst = lax.rem(me + o, n)
        for c in range(cap):
            outgoing[dst, c] = latent[in_slots[dst * cap + c]]
        latent_copy(o).start()

    for c in range(cap):
        fetched[me * cap + c] = latent[in_slots[me * cap + c]]

    outbox[...] = jnp.zeros_like(outbox)
    load_diag.wait()
    keep = lax.broadcasted_iota(jnp.int32, (width, width), 0) >= lax.broadcasted_iota(
        jnp.int32, (width, width), 1
    )

    @pl.loop(0, rows)
    def _(r):
        lower[r] = jnp.where(keep, lower[r], jnp.zeros((width, width), bf16))

    load_cond.wait()

    @pl.loop(1, n)
    def _(o):
        latent_copy(o).wait_recv()

    @pl.loop(0, rows, unroll=2)
    def _(r):
        own = fetched[pick[4 * r]]
        white = lax.dot_general(own, lower[r], NT, preferred_element_type=f32)
        for k in range(3):
            panel = fetched[pick[4 * r + k + 1]]
            white = white + lax.dot_general(panel, near[r, k], NT, preferred_element_type=f32)
        scored = (freedom + 1.0) * white / (freedom + white * white)
        low = scored.astype(bf16).astype(f32)
        sums[pl.ds(r, 1)] = jnp.sum(low, axis=0, keepdims=True)
        sums[pl.ds(rows + r, 1)] = jnp.sum(own.astype(f32), axis=0, keepdims=True)

    swap = pltpu.make_async_remote_copy(
        src_ref=sums,
        dst_ref=sums_in,
        send_sem=pair_sem.at[0],
        recv_sem=pair_sem.at[1],
        device_id=partner,
        device_id_type=MESH,
    )
    swap.start()
    swap.wait()
    sums_in[...] = sums_in[...] + sums[...]

    column = pl.ds(pl.multiple_of(core * half, half), half)
    place = lax.broadcasted_iota(jnp.int32, (16, width), 0)

    @pl.loop(0, rows, unroll=2)
    def _(r):
        total = jnp.broadcast_to(sums_in[pl.ds(r, 1)], (16, width))
        high = total.astype(bf16).astype(f32)
        parts = jnp.where(place == 0, high, jnp.where(place == 1, total - high, 0.0)).astype(bf16)
        back = jnp.dot(parts, lower[r, :, column], preferred_element_type=f32)
        back = jnp.sum(back, axis=0, keepdims=True)
        likely = noise[0] * (2 * draws * obs[pl.ds(r, 1)] - sums_in[pl.ds(rows + r, 1)])
        likely = jnp.where(core == 0, likely[:, :half], likely[:, half:])
        terms[pl.ds(4 * r, 1)] = (likely - back) * inverse_draws
        for k in range(3):
            back = jnp.dot(parts, near[r, k, :, column], preferred_element_type=f32)
            back = jnp.sum(back, axis=0, keepdims=True)
            terms[pl.ds(4 * r + k + 1, 1)] = -back * inverse_draws

    def term_copy(o):
        dst = lax.rem(me + o, n)
        return pltpu.make_async_remote_copy(
            src_ref=outbox.at[dst],
            dst_ref=inbox.at[me],
            send_sem=term_send.at[o],
            recv_sem=term_recv.at[o],
            device_id=(dst, core),
            device_id_type=MESH,
        )

    @pl.loop(1, n)
    def _(o):
        dst = lax.rem(me + o, n)
        for c in range(cap):
            outbox[dst, pl.ds(c, 1)] = terms[pl.ds(inverse[dst * cap + c], 1)]
        term_copy(o).start()

    for c in range(cap):
        outbox[me, pl.ds(c, 1)] = terms[pl.ds(inverse[me * cap + c], 1)]
    inbox[me] = outbox[me]

    slots = out.shape[0]
    hits = lax.broadcasted_iota(jnp.int32, (slots, n * pad), 0) == target[...]
    hits = jnp.where(hits, 1.0, 0.0).astype(bf16)

    @pl.loop(1, n)
    def _(o):
        term_copy(o).wait_recv()

    arrived = inbox[...].reshape(n * pad, half)
    first = arrived.astype(bf16)
    rest = arrived - first.astype(f32)
    second = rest.astype(bf16)
    third = (rest - second.astype(f32)).astype(bf16)
    total = jnp.dot(hits, first, preferred_element_type=f32)
    total = total + jnp.dot(hits, second, preferred_element_type=f32)
    out[...] = total + jnp.dot(hits, third, preferred_element_type=f32)

    @pl.loop(1, n)
    def _(o):
        latent_copy(o).wait_send()
        term_copy(o).wait_send()


def body(batch_ids, cond_ids, home, latent, diag_factor, cond_factor, obs, noise_prec):
    n = lax.axis_size("blk")
    me = lax.axis_index("blk")
    per_owner, draws, width = latent.shape
    rows = batch_ids.shape[0]
    want = 4 * rows
    cap = max(2, 10 * rows // n)
    pad = -(-cap // 8) * 8
    block_ids = jnp.concatenate([batch_ids[:, None], cond_ids], axis=1).reshape(-1)
    wanted = home[block_ids]
    every = lax.all_gather(wanted, "blk")
    rank_of = jnp.arange(cap)

    before = jnp.arange(want)[:, None] < jnp.arange(want)[None, :]
    mine = every // per_owner == me
    rank = jnp.dot(mine.astype(bf16), before.astype(bf16), preferred_element_type=f32)
    rank = jnp.where(mine, rank.astype(jnp.int32), -1)
    hit = rank[:, None, :] == rank_of[None, :, None]
    in_slots = jnp.sum(jnp.where(hit, (every % per_owner + 1)[:, None, :], 0), axis=2) - 1
    target = jnp.pad(in_slots, ((0, 0), (0, pad - cap)), constant_values=-1).reshape(1, n * pad)

    owner = wanted // per_owner
    same = owner[:, None] == owner[None, :]
    own_rank = jnp.sum((same & before).astype(jnp.int32), axis=0)
    pick = owner * cap + own_rank
    spot = jnp.arange(n * cap)
    inverse = jnp.sum(
        jnp.where(pick[None, :] == spot[:, None], jnp.arange(want)[None, :], 0), axis=1
    )

    smem = pl.BlockSpec(memory_space=pltpu.SMEM)
    vmem = pl.BlockSpec(memory_space=pltpu.VMEM)
    anywhere = pl.BlockSpec(memory_space=pl.ANY)
    return pl.pallas_call(
        functools.partial(kernel, n, cap),
        out_shape=jax.ShapeDtypeStruct((per_owner, width // 2), f32),
        in_specs=[smem, smem, smem, vmem, smem, vmem, anywhere, anywhere, vmem],
        out_specs=vmem,
        scratch_shapes=[
            pltpu.VMEM((n, cap, draws, width), bf16),
            pltpu.VMEM((n * cap, draws, width), bf16),
            pltpu.VMEM(diag_factor.shape, bf16),
            pltpu.VMEM(cond_factor.shape, bf16),
            pltpu.VMEM((2 * rows, width), f32),
            pltpu.VMEM((2 * rows, width), f32),
            pltpu.VMEM((want, width // 2), f32),
            pltpu.VMEM((n, pad, width // 2), f32),
            pltpu.VMEM((n, pad, width // 2), f32),
            pltpu.SemaphoreType.DMA((2,)),
            pltpu.SemaphoreType.DMA((n,)),
            pltpu.SemaphoreType.DMA((n,)),
            pltpu.SemaphoreType.DMA((2,)),
            pltpu.SemaphoreType.DMA((n,)),
            pltpu.SemaphoreType.DMA((n,)),
        ],
        compiler_params=pltpu.CompilerParams(
            collective_id=0, has_side_effects=True, vmem_limit_bytes=56 * 1024 * 1024
        ),
    )(
        jnp.maximum(in_slots, 0).reshape(-1),
        pick,
        inverse,
        target,
        noise_prec.reshape(1),
        latent,
        diag_factor,
        cond_factor,
        obs,
    )


def solution(mesh):
    placed = (
        P("blk"),
        P("blk", None),
        P(),
        P("blk", "mc", None),
        P("blk", None, None),
        P("blk", None, None, None),
        P("blk", None),
        P(),
    )
    return jax.shard_map(
        body, mesh=mesh, in_specs=placed, out_specs=P("blk", "mc"), check_vma=False
    )
```

time: 148 us -> 125 us (0.84)
  Pallas kernels: 0 us -> 75.6 us
  waiting for transfers between devices: 68 us -> 0 us
  blocking collectives: 15.4 us -> 42.2 us
  matrix products: 17.1 us -> 0.14 us
  starting transfers between devices: 16.4 us -> 0 us
  between operations: 14.3 us -> 0.74 us
  local copies, waits for them, and re-layouts: 11 us -> 4.43 us
  other arithmetic: 5 us -> 1.98 us
    pallas_call x0 -> x1, Pallas kernels: none -> 75.6 us  [body(): pl.pallas_call(functools.partial(kernel, n, cap), out_shape=jax.ShapeDtyp...]
    all_to_all x2 -> x0, waiting for transfers between devices: 62.1 us -> none  [the longest x1 50.5 us: body(): lax.all_to_all(outgoing, 'blk', split_axis=0, concat_axis=0, tiled=True)]
    all_gather x0 -> x1, blocking collectives: none -> 42.2 us  [body(): every = lax.all_gather(wanted, 'blk')]
    dot_general x4 -> x1, matrix products: 17.1 us -> 0.14 us  [body(): jnp.dot(mine.astype(bf16), before.astype(bf16), preferred_element_type=f32)]
    all_to_all x2 -> x0, starting transfers between devices: 16.3 us -> none  [the longest x1 11.9 us: body(): lax.all_to_all(outbox_terms.reshape(owners, capacity, block_width), 'blk'...]
    all_to_all x1 -> x0, blocking collectives: 15.4 us -> none  [body(): lax.all_to_all(outbox, 'blk', split_axis=0, concat_axis=0, tiled=True)]
    reduce_scatter x1 -> x0, waiting for transfers between devices: 5.85 us -> none  [body(): return lax.psum_scatter(stored, 'mc', scatter_dimension=1, tiled=True)]
    gather x2 -> x0, local copies, waits for them, and re-layouts: 5.42 us -> none  [the longest x1 3.04 us: body(): outgoing = latent[jnp.maximum(in_slots, 0)]]
  transfers between devices with their start and end apart: 3 -> 0, of which waited for: 3 -> 0; matrix products, arithmetic and copies ran while one was open for 0% -> 0% of each run, Pallas kernels for 0% -> 0%
where the time goes in v1:
time: 125 us
  Pallas kernels  75.6 us (60%)
  blocking collectives  42.2 us (34%)
  local copies, waits for them, and re-layouts  4.43 us (4%)
  other arithmetic  1.98 us (2%)
    pallas_call x1, Pallas kernels, body(): pl.pallas_call(functools.partial(kernel, n, cap), out_shape=jax.ShapeDtyp...  75.6 us
    all_gather x1, blocking collectives, body(): every = lax.all_gather(wanted, 'blk')  42.2 us

profile of v1, /device:TPU:0, one launch (start us, length us, event | category | flops | bytes accessed | tf_op | source)
XLA Modules:
  0.0 125.0 jit_solution(18079232973080173892)
XLA Ops:
  0.0 0.0 copy-start
  0.7 0.7 pad_add_fusion
  1.4 0.1 copy.16
  1.4 0.1 reshape.85
  1.6 0.0 copy-done
  1.6 1.1 gather_fusion
  2.8 0.1 convert_reduce_fusion
  2.9 0.0 copy-start.1
  2.9 0.7 select_reduce_fusion.inverse
  3.6 42.2 %all-gather.1 = s32[16,1,128]{2,1,0:T(1,128)S(1)} all-gather(s32[1,1,128]{2,1,0:T(1,128)S(1)} %bitcast.9), channel_id=2, replica_groups=mesh['blk'=16,'mc'=2] {'blk'}, dimensions={0}, use_global_device_ids=true | all-gather | bytes 8704 | tf_op jit(solution)/shard_map/all_gather | solution.py:206
  45.8 0.1 fusion
  45.9 0.4 select_reduce_fusion.1
  46.4 0.1 copy.19
  46.5 0.7 reshape.86.target
  47.1 0.1 copy.17
  47.2 0.7 max.12.in_slots
  47.9 0.0 copy-done.1
  47.9 75.6 %shard_map.82 = f32[256,128]{1,0:T(8,128)} custom-call(s32[320]{0:T(512)} %max.12.in_slots, s32[128]{0:T(128)} %copy-done.1, s32[320]{0:T(512)} %select_reduce_fusion.inverse, s32[1,384]{1,0:T(1,128)} %reshape.86.target, f32[1]{0:T(128)} %bitcast.6.noise, bf16[256,16,256]{2,1,0:T(8,128)(2,1)} %latent.1, bf16[32,256,256]{2,1,0:T(8,128)(2,1)} %diag.1, ...), custom_call_target="tpu_custom_call" | custom-call | tf_op jit(solution)/shard_map/pallas_call | solution.py:229
  123.5 1.6 %copy.22 = f32[256,128]{1,0:T(8,128)} copy(f32[256,128]{1,0:T(8,128)} %shard_map.82) | data formatting | bytes 262144
  (7 shorter events, 0.1 us)
Async XLA Ops:
  0.0 1.6 %copy-start = (s32[4096]{0:T(1024)S(1)}, s32[4096]{0:T(1024)}, u32[]{:S(2)}) copy-start(s32[4096]{0:T(1024)} %param.10) | copy-start | bytes 49156
  2.9 45.0 %copy-start.1 = (s32[128]{0:T(128)}, s32[128]{0:T(128)S(1)}, u32[]{:S(2)}) copy-start(s32[128]{0:T(128)S(1)} %multiply_add_fusion.pick) | copy-start | bytes 1540

commit v2 on v1

v2 whole, which is shorter than its diff:
```python
import functools

import jax
import jax.numpy as jnp
from jax import lax
from jax.experimental import pallas as pl
from jax.experimental.pallas import tpu as pltpu
from jax.sharding import PartitionSpec as P

freedom = 4.0
MESH = pl.DeviceIdType.MESH
f32 = jnp.float32
bf16 = jnp.bfloat16
NT = (((1,), (1,)), ((), ()))


def kernel(
    n,
    cap,
    wanted,
    noise,
    latent_any,
    diag,
    cond,
    obs,
    out,
    every,
    tables,
    scalars,
    latent,
    outgoing,
    fetched_left,
    fetched_right,
    lower,
    near,
    partial,
    sums,
    sums_in,
    terms,
    outbox,
    inbox,
    load_sem,
    id_send,
    id_recv,
    lat_send,
    lat_recv,
    pair_sem,
    term_send,
    term_recv,
):
    fetched = (fetched_left, fetched_right)
    rows = obs.shape[0]
    want = 4 * rows
    per_owner, draws, width = latent.shape
    half = width // 2
    me = lax.axis_index("blk")
    core = lax.axis_index("mc")
    partner = (me, 1 - core)
    inverse_draws = 1.0 / (2 * draws)

    load_latent = pltpu.make_async_copy(latent_any, latent, load_sem.at[2])
    load_diag = pltpu.make_async_copy(diag, lower, load_sem.at[0])
    load_cond = pltpu.make_async_copy(cond, near, load_sem.at[1])
    load_latent.start()
    load_diag.start()
    load_cond.start()

    barrier = pltpu.get_barrier_semaphore()

    @pl.loop(1, n)
    def _(o):
        pl.semaphore_signal(
            barrier, inc=1, device_id=(lax.rem(me + o, n), core), device_id_type=MESH
        )

    pl.semaphore_signal(barrier, inc=1, device_id=partner, device_id_type=MESH)
    pl.semaphore_wait(barrier, n)

    def id_copy(o):
        return pltpu.make_async_remote_copy(
            src_ref=wanted,
            dst_ref=every.at[me],
            send_sem=id_send.at[o],
            recv_sem=id_recv.at[o],
            device_id=(lax.rem(me + o, n), core),
            device_id_type=MESH,
        )

    @pl.loop(1, n)
    def _(o):
        id_copy(o).start()

    every[me] = wanted[...]
    lane = lax.broadcasted_iota(jnp.int32, (n, want), 1)
    owner = lax.broadcasted_iota(jnp.int32, (n, want), 0)

    def ranks(mask):
        count = jnp.where(mask, 1, 0)
        shift = 1
        while shift < want:
            count = count + jnp.where(lane >= shift, pltpu.roll(count, shift, 1), 0)
            shift *= 2
        return count - 1

    def table(mask, rank, value):
        rank = jnp.where(mask, rank, -1)
        filled = jnp.zeros((n, want), jnp.int32)
        for c in range(cap):
            found = jnp.sum(jnp.where(rank == c, value, 0), axis=1, keepdims=True)
            filled = jnp.where(lane == c, found, filled)
        return filled

    mine = jnp.broadcast_to(wanted[...], (n, want)) - owner * per_owner
    mine = (mine >= 0) & (mine < per_owner)
    rank = ranks(mine)
    tables[pl.ds(n, n)] = table(mine, rank, lane)
    spot = jnp.sum(jnp.where(mine, owner * cap + rank, 0), axis=0, keepdims=True)
    tables[pl.ds(2 * n, 8)] = jnp.broadcast_to(spot, (8, want))

    @pl.loop(1, n)
    def _(o):
        id_copy(o).wait_recv()

    slot = every[...].reshape(n, want) - me * per_owner
    mine = (slot >= 0) & (slot < per_owner)
    tables[pl.ds(0, n)] = table(mine, ranks(mine), slot + 1) - 1
    to_scalars = pltpu.make_async_copy(tables, scalars, load_sem.at[3])
    to_scalars.start()
    load_latent.wait()
    to_scalars.wait()

    def slot_of(owner, c):
        return jnp.maximum(scalars[owner, c], 0)

    def term_of(owner, c):
        return scalars[n + owner, c]

    def panel_of(w):
        return scalars[2 * n, w]

    def latent_copy(h, o):
        dst = lax.rem(me + o, n)
        return pltpu.make_async_remote_copy(
            src_ref=outgoing.at[h, dst],
            dst_ref=fetched[h].at[pl.ds(me * cap, cap)],
            send_sem=lat_send.at[h * n + o],
            recv_sem=lat_recv.at[h * n + o],
            device_id=(dst, core),
            device_id_type=MESH,
        )

    for h in range(2):
        part = slice(h * half, (h + 1) * half)

        @pl.loop(1, n)
        def _(o):
            dst = lax.rem(me + o, n)
            for c in range(cap):
                outgoing[h, dst, c] = latent[slot_of(dst, c), :, part]
            latent_copy(h, o).start()

    for h in range(2):
        part = slice(h * half, (h + 1) * half)
        for c in range(cap):
            fetched[h][me * cap + c] = latent[slot_of(me, c), :, part]

    outbox[...] = jnp.zeros_like(outbox)
    load_diag.wait()
    keep = lax.broadcasted_iota(jnp.int32, (width, width), 0) >= lax.broadcasted_iota(
        jnp.int32, (width, width), 1
    )

    @pl.loop(0, rows)
    def _(r):
        lower[r] = jnp.where(keep, lower[r], jnp.zeros((width, width), bf16))

    load_cond.wait()

    def product(h, r):
        part = slice(h * half, (h + 1) * half)
        panels = [fetched[h][panel_of(4 * r + k)] for k in range(4)]
        blocks = [lower[r, :, part]] + [near[r, k, :, part] for k in range(3)]
        return lax.dot_general(
            jnp.concatenate(panels, axis=1),
            jnp.concatenate(blocks, axis=1),
            NT,
            preferred_element_type=f32,
        )

    @pl.loop(1, n)
    def _(o):
        latent_copy(0, o).wait_recv()

    @pl.loop(0, rows, unroll=4)
    def _(r):
        partial[r] = product(0, r)

    @pl.loop(1, n)
    def _(o):
        latent_copy(1, o).wait_recv()

    @pl.loop(0, rows, unroll=4)
    def _(r):
        white = partial[r] + product(1, r)
        scored = (freedom + 1.0) * white / (freedom + white * white)
        low = scored.astype(bf16).astype(f32)
        sums[pl.ds(r, 1)] = jnp.sum(low, axis=0, keepdims=True)
        spot = panel_of(4 * r)
        own = jnp.concatenate([fetched_left[spot], fetched_right[spot]], axis=1).astype(f32)
        sums[pl.ds(rows + r, 1)] = jnp.sum(own, axis=0, keepdims=True)

    swap = pltpu.make_async_remote_copy(
        src_ref=sums,
        dst_ref=sums_in,
        send_sem=pair_sem.at[0],
        recv_sem=pair_sem.at[1],
        device_id=partner,
        device_id_type=MESH,
    )
    swap.start()
    swap.wait()
    sums_in[...] = sums_in[...] + sums[...]

    column = pl.ds(pl.multiple_of(core * half, half), half)
    place = lax.broadcasted_iota(jnp.int32, (16, width), 0)

    @pl.loop(0, rows, unroll=4)
    def _(r):
        total = jnp.broadcast_to(sums_in[pl.ds(r, 1)], (16, width))
        high = total.astype(bf16).astype(f32)
        parts = jnp.where(place == 0, high, jnp.where(place == 1, total - high, 0.0)).astype(bf16)
        back = jnp.dot(parts, lower[r, :, column], preferred_element_type=f32)
        back = jnp.sum(back, axis=0, keepdims=True)
        likely = noise[0] * (2 * draws * obs[pl.ds(r, 1)] - sums_in[pl.ds(rows + r, 1)])
        likely = jnp.where(core == 0, likely[:, :half], likely[:, half:])
        terms[pl.ds(4 * r, 1)] = (likely - back) * inverse_draws
        for k in range(3):
            back = jnp.dot(parts, near[r, k, :, column], preferred_element_type=f32)
            back = jnp.sum(back, axis=0, keepdims=True)
            terms[pl.ds(4 * r + k + 1, 1)] = -back * inverse_draws

    def term_copy(o):
        dst = lax.rem(me + o, n)
        return pltpu.make_async_remote_copy(
            src_ref=outbox.at[dst],
            dst_ref=inbox.at[me],
            send_sem=term_send.at[o],
            recv_sem=term_recv.at[o],
            device_id=(dst, core),
            device_id_type=MESH,
        )

    @pl.loop(1, n)
    def _(o):
        dst = lax.rem(me + o, n)
        for c in range(cap):
            outbox[dst, pl.ds(c, 1)] = terms[pl.ds(term_of(dst, c), 1)]
        term_copy(o).start()

    for c in range(cap):
        outbox[me, pl.ds(c, 1)] = terms[pl.ds(term_of(me, c), 1)]
    inbox[me] = outbox[me]
    pad = outbox.shape[1]
    place = lax.broadcasted_iota(jnp.int32, (per_owner, want), 0)

    def collect(source):
        hits = jnp.where(place == tables[pl.ds(source, 1)], 1.0, 0.0).astype(bf16)[:, :pad]
        arrived = inbox[source]
        first = arrived.astype(bf16)
        rest = arrived - first.astype(f32)
        second = rest.astype(bf16)
        third = (rest - second.astype(f32)).astype(bf16)
        total = jnp.dot(hits, first, preferred_element_type=f32)
        total = total + jnp.dot(hits, second, preferred_element_type=f32)
        return total + jnp.dot(hits, third, preferred_element_type=f32)

    out[...] = collect(me)

    @pl.loop(1, n)
    def _(o):
        term_copy(o).wait_recv()
        out[...] += collect(lax.rem(me - o + n, n))

    @pl.loop(1, n)
    def _(o):
        id_copy(o).wait_send()
        latent_copy(0, o).wait_send()
        latent_copy(1, o).wait_send()
        term_copy(o).wait_send()


def body(batch_ids, cond_ids, home, latent, diag_factor, cond_factor, obs, noise_prec):
    n = lax.axis_size("blk")
    per_owner, draws, width = latent.shape
    rows = batch_ids.shape[0]
    want = 4 * rows
    cap = max(2, 10 * rows // n)
    pad = -(-cap // 8) * 8
    block_ids = jnp.concatenate([batch_ids[:, None], cond_ids], axis=1).reshape(-1)
    wanted = home[block_ids].reshape(1, want)

    smem = pl.BlockSpec(memory_space=pltpu.SMEM)
    vmem = pl.BlockSpec(memory_space=pltpu.VMEM)
    anywhere = pl.BlockSpec(memory_space=pl.ANY)
    return pl.pallas_call(
        functools.partial(kernel, n, cap),
        out_shape=jax.ShapeDtypeStruct((per_owner, width // 2), f32),
        in_specs=[vmem, smem, anywhere, anywhere, anywhere, vmem],
        out_specs=vmem,
        scratch_shapes=[
            pltpu.VMEM((n, 1, want), jnp.int32),
            pltpu.VMEM((2 * n + 8, want), jnp.int32),
            pltpu.SMEM((2 * n + 8, want), jnp.int32),
            pltpu.VMEM(latent.shape, bf16),
            pltpu.VMEM((2, n, cap, draws, width // 2), bf16),
            pltpu.VMEM((n * cap, draws, width // 2), bf16),
            pltpu.VMEM((n * cap, draws, width // 2), bf16),
            pltpu.VMEM(diag_factor.shape, bf16),
            pltpu.VMEM(cond_factor.shape, bf16),
            pltpu.VMEM((rows, draws, width), f32),
            pltpu.VMEM((2 * rows, width), f32),
            pltpu.VMEM((2 * rows, width), f32),
            pltpu.VMEM((want, width // 2), f32),
            pltpu.VMEM((n, pad, width // 2), f32),
            pltpu.VMEM((n, pad, width // 2), f32),
            pltpu.SemaphoreType.DMA((4,)),
            pltpu.SemaphoreType.DMA((n,)),
            pltpu.SemaphoreType.DMA((n,)),
            pltpu.SemaphoreType.DMA((2 * n,)),
            pltpu.SemaphoreType.DMA((2 * n,)),
            pltpu.SemaphoreType.DMA((2,)),
            pltpu.SemaphoreType.DMA((n,)),
            pltpu.SemaphoreType.DMA((n,)),
        ],
        compiler_params=pltpu.CompilerParams(
            collective_id=0, has_side_effects=True, vmem_limit_bytes=56 * 1024 * 1024
        ),
    )(wanted, noise_prec.reshape(1), latent, diag_factor, cond_factor, obs)


def solution(mesh):
    placed = (
        P("blk"),
        P("blk", None),
        P(),
        P("blk", "mc", None),
        P("blk", None, None),
        P("blk", None, None, None),
        P("blk", None),
        P(),
    )
    return jax.shard_map(
        body, mesh=mesh, in_specs=placed, out_specs=P("blk", "mc"), check_vma=False
    )
```

time: 125 us -> 92 us (0.74)
  blocking collectives: 42.2 us -> 0 us
  Pallas kernels: 75.6 us -> 86.9 us
  other arithmetic: 1.98 us -> 0.7 us
    all_gather x1 -> x0, blocking collectives: 42.2 us -> none  [body(): every = lax.all_gather(wanted, 'blk')]
    pallas_call x1, Pallas kernels: 75.6 us -> 86.9 us  [body(): pl.pallas_call(functools.partial(kernel, n, cap), out_shape=jax.ShapeDtyp...]
where the time goes in v2:
time: 92 us; the launch traced here: 91.7 us
  Pallas kernels  86.9 us (94%)
  local copies, waits for them, and re-layouts  3.44 us (4%)
    pallas_call x1, Pallas kernels, body(): pl.pallas_call(functools.partial(kernel, n, cap), out_shape=jax.ShapeDtyp...  86.9 us

profile of v2, /device:TPU:0, one launch (start us, length us, event | category | flops | bytes accessed | tf_op | source)
XLA Modules:
  0.0 91.7 jit_solution(1763109560729307691)
XLA Ops:
  0.0 0.0 copy-start
  0.7 0.7 pad_add_fusion
  1.4 0.1 copy.10
  1.4 0.1 reshape.37
  1.6 0.0 copy-done
  1.6 1.7 %gather_fusion = s32[128]{0:T(128)} fusion(s32[4096]{0:T(1024)S(1)} %copy-done, s32[1024]{0:T(1024)S(1)} %pad_clamp_fusion), kind=kCustom, calls=%fused_computation | custom fusion | bytes 1536 | tf_op jit(solution)/shard_map/gather | solution.py:300
  3.3 86.9 %shard_map.82 = f32[256,128]{1,0:T(8,128)} custom-call(s32[1,128]{1,0:T(1,128)} %bitcast.6, f32[1]{0:T(128)} %bitcast.5.noise, bf16[256,16,256]{2,1,0:T(8,128)(2,1)} %latent_any.1, bf16[32,256,256]{2,1,0:T(8,128)(2,1)} %diag.1, bf16[32,3,256,256]{3,2,1,0:T(8,128)(2,1)} %cond.1, f32[32,256]{1,0:T(8,128)} %obs.1), custom_call_target="tpu_custom_call" | custom-call | tf_op jit(solution)/shard_map/pallas_call | solution.py:305
  90.2 1.6 %copy.13 = f32[256,128]{1,0:T(8,128)} copy(f32[256,128]{1,0:T(8,128)} %shard_map.82) | data formatting | bytes 262144
  (2 shorter events, 0.0 us)
Async XLA Ops:
  0.0 1.6 %copy-start = (s32[4096]{0:T(1024)S(1)}, s32[4096]{0:T(1024)}, u32[]{:S(2)}) copy-start(s32[4096]{0:T(1024)} %param.10) | copy-start | bytes 49156

commit v3 on v2

--- a/solution.py
+++ b/solution.py
@@ -58,6 +58,16 @@
     partner = (me, 1 - core)
     inverse_draws = 1.0 / (2 * draws)
 
+    def peer(o):
+        bit, other = 1, 0
+        while bit < n:
+            other = other + lax.rem(me // bit + o // bit, 2) * bit
+            bit *= 2
+        return other
+
+    def turn(k):
+        return lax.rem(k + 1, 2) * (n // 2) + (k + 1) // 2
+
     load_latent = pltpu.make_async_copy(latent_any, latent, load_sem.at[2])
     load_diag = pltpu.make_async_copy(diag, lower, load_sem.at[0])
     load_cond = pltpu.make_async_copy(cond, near, load_sem.at[1])
@@ -70,7 +80,7 @@
     @pl.loop(1, n)
     def _(o):
         pl.semaphore_signal(
-            barrier, inc=1, device_id=(lax.rem(me + o, n), core), device_id_type=MESH
+            barrier, inc=1, device_id=(peer(o), core), device_id_type=MESH
         )
 
     pl.semaphore_signal(barrier, inc=1, device_id=partner, device_id_type=MESH)
@@ -82,7 +92,7 @@
             dst_ref=every.at[me],
             send_sem=id_send.at[o],
             recv_sem=id_recv.at[o],
-            device_id=(lax.rem(me + o, n), core),
+            device_id=(peer(o), core),
             device_id_type=MESH,
         )
 
@@ -139,7 +149,7 @@
         return scalars[2 * n, w]
 
     def latent_copy(h, o):
-        dst = lax.rem(me + o, n)
+        dst = peer(o)
         return pltpu.make_async_remote_copy(
             src_ref=outgoing.at[h, dst],
             dst_ref=fetched[h].at[pl.ds(me * cap, cap)],
@@ -149,15 +159,16 @@
             device_id_type=MESH,
         )
 
-    for h in range(2):
+    def pack(h, o):
+        dst = peer(o)
         part = slice(h * half, (h + 1) * half)
-
-        @pl.loop(1, n)
-        def _(o):
-            dst = lax.rem(me + o, n)
-            for c in range(cap):
-                outgoing[h, dst, c] = latent[slot_of(dst, c), :, part]
-            latent_copy(h, o).start()
+        for c in range(cap):
+            outgoing[h, dst, c] = latent[slot_of(dst, c), :, part]
+        latent_copy(h, o).start()
+
+    @pl.loop(0, n - 1)
+    def _(k):
+        pack(0, turn(k))
 
     for h in range(2):
         part = slice(h * half, (h + 1) * half)
@@ -173,6 +184,11 @@
     @pl.loop(0, rows)
     def _(r):
         lower[r] = jnp.where(keep, lower[r], jnp.zeros((width, width), bf16))
+
+    @pl.loop(0, n - 1)
+    def _(k):
+        latent_copy(0, turn(k)).wait_send()
+        pack(1, turn(k))
 
     load_cond.wait()
 
@@ -199,48 +215,58 @@
     def _(o):
         latent_copy(1, o).wait_recv()
 
-    @pl.loop(0, rows, unroll=4)
-    def _(r):
-        white = partial[r] + product(1, r)
-        scored = (freedom + 1.0) * white / (freedom + white * white)
-        low = scored.astype(bf16).astype(f32)
-        sums[pl.ds(r, 1)] = jnp.sum(low, axis=0, keepdims=True)
-        spot = panel_of(4 * r)
-        own = jnp.concatenate([fetched_left[spot], fetched_right[spot]], axis=1).astype(f32)
-        sums[pl.ds(rows + r, 1)] = jnp.sum(own, axis=0, keepdims=True)
-
-    swap = pltpu.make_async_remote_copy(
-        src_ref=sums,
-        dst_ref=sums_in,
-        send_sem=pair_sem.at[0],
-        recv_sem=pair_sem.at[1],
-        device_id=partner,
-        device_id_type=MESH,
-    )
-    swap.start()
-    swap.wait()
-    sums_in[...] = sums_in[...] + sums[...]
-
+    group = rows // 2
     column = pl.ds(pl.multiple_of(core * half, half), half)
     place = lax.broadcasted_iota(jnp.int32, (16, width), 0)
 
-    @pl.loop(0, rows, unroll=4)
-    def _(r):
-        total = jnp.broadcast_to(sums_in[pl.ds(r, 1)], (16, width))
-        high = total.astype(bf16).astype(f32)
-        parts = jnp.where(place == 0, high, jnp.where(place == 1, total - high, 0.0)).astype(bf16)
-        back = jnp.dot(parts, lower[r, :, column], preferred_element_type=f32)
-        back = jnp.sum(back, axis=0, keepdims=True)
-        likely = noise[0] * (2 * draws * obs[pl.ds(r, 1)] - sums_in[pl.ds(rows + r, 1)])
-        likely = jnp.where(core == 0, likely[:, :half], likely[:, half:])
-        terms[pl.ds(4 * r, 1)] = (likely - back) * inverse_draws
-        for k in range(3):
-            back = jnp.dot(parts, near[r, k, :, column], preferred_element_type=f32)
+    def swap(g):
+        return pltpu.make_async_remote_copy(
+            src_ref=sums.at[g],
+            dst_ref=sums_in.at[g],
+            send_sem=pair_sem.at[g],
+            recv_sem=pair_sem.at[2 + g],
+            device_id=partner,
+            device_id_type=MESH,
+        )
+
+    for g in range(2):
+
+        @pl.loop(0, group, unroll=4)
+        def _(i):
+            r = g * group + i
+            white = partial[r] + product(1, r)
+            scored = (freedom + 1.0) * white / (freedom + white * white)
+            low = scored.astype(bf16).astype(f32)
+            sums[g, pl.ds(i, 1)] = jnp.sum(low, axis=0, keepdims=True)
+            spot = panel_of(4 * r)
+            own = jnp.concatenate([fetched_left[spot], fetched_right[spot]], axis=1).astype(f32)
+            sums[g, pl.ds(group + i, 1)] = jnp.sum(own, axis=0, keepdims=True)
+
+        swap(g).start()
+
+    for g in range(2):
+        swap(g).wait_recv()
+        sums_in[g] = sums_in[g] + sums[g]
+
+        @pl.loop(0, group, unroll=4)
+        def _(i):
+            r = g * group + i
+            total = jnp.broadcast_to(sums_in[g, pl.ds(i, 1)], (16, width))
+            high = total.astype(bf16).astype(f32)
+            parts = jnp.where(place == 0, high, jnp.where(place == 1, total - high, 0.0)).astype(bf16)
+            back = jnp.dot(parts, lower[r, :, column], preferred_element_type=f32)
             back = jnp.sum(back, axis=0, keepdims=True)
-            terms[pl.ds(4 * r + k + 1, 1)] = -back * inverse_draws
+            own = sums_in[g, pl.ds(group + i, 1)]
+            likely = noise[0] * (2 * draws * obs[pl.ds(r, 1)] - own)
+            likely = jnp.where(core == 0, likely[:, :half], likely[:, half:])
+            terms[pl.ds(4 * r, 1)] = (likely - back) * inverse_draws
+            for k in range(3):
+                back = jnp.dot(parts, near[r, k, :, column], preferred_element_type=f32)
+                back = jnp.sum(back, axis=0, keepdims=True)
+                terms[pl.ds(4 * r + k + 1, 1)] = -back * inverse_draws
 
     def term_copy(o):
-        dst = lax.rem(me + o, n)
+        dst = peer(o)
         return pltpu.make_async_remote_copy(
             src_ref=outbox.at[dst],
             dst_ref=inbox.at[me],
@@ -250,9 +276,10 @@
             device_id_type=MESH,
         )
 
-    @pl.loop(1, n)
-    def _(o):
-        dst = lax.rem(me + o, n)
+    @pl.loop(0, n - 1)
+    def _(k):
+        o = turn(k)
+        dst = peer(o)
         for c in range(cap):
             outbox[dst, pl.ds(c, 1)] = terms[pl.ds(term_of(dst, c), 1)]
         term_copy(o).start()
@@ -279,14 +306,16 @@
     @pl.loop(1, n)
     def _(o):
         term_copy(o).wait_recv()
-        out[...] += collect(lax.rem(me - o + n, n))
+        out[...] += collect(peer(o))
 
     @pl.loop(1, n)
     def _(o):
         id_copy(o).wait_send()
-        latent_copy(0, o).wait_send()
         latent_copy(1, o).wait_send()
         term_copy(o).wait_send()
+
+    swap(0).wait_send()
+    swap(1).wait_send()
 
 
 def body(batch_ids, cond_ids, home, latent, diag_factor, cond_factor, obs, noise_prec):
@@ -318,8 +347,8 @@
             pltpu.VMEM(diag_factor.shape, bf16),
             pltpu.VMEM(cond_factor.shape, bf16),
             pltpu.VMEM((rows, draws, width), f32),
-            pltpu.VMEM((2 * rows, width), f32),
-            pltpu.VMEM((2 * rows, width), f32),
+            pltpu.VMEM((2, rows, width), f32),
+            pltpu.VMEM((2, rows, width), f32),
             pltpu.VMEM((want, width // 2), f32),
             pltpu.VMEM((n, pad, width // 2), f32),
             pltpu.VMEM((n, pad, width // 2), f32),
@@ -328,7 +357,7 @@
             pltpu.SemaphoreType.DMA((n,)),
             pltpu.SemaphoreType.DMA((2 * n,)),
             pltpu.SemaphoreType.DMA((2 * n,)),
-            pltpu.SemaphoreType.DMA((2,)),
+            pltpu.SemaphoreType.DMA((4,)),
             pltpu.SemaphoreType.DMA((n,)),
             pltpu.SemaphoreType.DMA((n,)),
         ],

time: 92 us -> 89.6 us (0.974)
  Pallas kernels: 86.9 us -> 84.5 us
    pallas_call x1, Pallas kernels: 86.9 us -> 84.5 us  [body(): pl.pallas_call(functools.partial(kernel, n, cap), out_shape=jax.ShapeDtyp...]
where the time goes in v3:
time: 89.6 us; the launch traced here: 89.3 us
  Pallas kernels  84.5 us (94%)
  local copies, waits for them, and re-layouts  3.44 us (4%)
    pallas_call x1, Pallas kernels, body(): pl.pallas_call(functools.partial(kernel, n, cap), out_shape=jax.ShapeDtyp...  84.5 us

profile of v3, /device:TPU:0, one launch (start us, length us, event | category | flops | bytes accessed | tf_op | source)
XLA Modules:
  0.0 89.3 jit_solution(1223358926417136101)
XLA Ops:
  0.0 0.0 copy-start
  0.7 0.7 pad_add_fusion
  1.4 0.1 copy.10
  1.4 0.1 reshape.37
  1.6 0.0 copy-done
  1.6 1.7 %gather_fusion = s32[128]{0:T(128)} fusion(s32[4096]{0:T(1024)S(1)} %copy-done, s32[1024]{0:T(1024)S(1)} %pad_clamp_fusion), kind=kCustom, calls=%fused_computation | custom fusion | bytes 1536 | tf_op jit(solution)/shard_map/gather | solution.py:329
  3.3 84.5 %shard_map.82 = f32[256,128]{1,0:T(8,128)} custom-call(s32[1,128]{1,0:T(1,128)} %bitcast.6, f32[1]{0:T(128)} %bitcast.5.noise, bf16[256,16,256]{2,1,0:T(8,128)(2,1)} %latent_any.1, bf16[32,256,256]{2,1,0:T(8,128)(2,1)} %diag.1, bf16[32,3,256,256]{3,2,1,0:T(8,128)(2,1)} %cond.1, f32[32,256]{1,0:T(8,128)} %obs.1), custom_call_target="tpu_custom_call" | custom-call | tf_op jit(solution)/shard_map/pallas_call | solution.py:334
  87.7 1.6 %copy.13 = f32[256,128]{1,0:T(8,128)} copy(f32[256,128]{1,0:T(8,128)} %shard_map.82) | data formatting | bytes 262144
  (2 shorter events, 0.0 us)
Async XLA Ops:
  0.0 1.6 %copy-start = (s32[4096]{0:T(1024)S(1)}, s32[4096]{0:T(1024)}, u32[]{:S(2)}) copy-start(s32[4096]{0:T(1024)} %param.10) | copy-start | bytes 49156

commit v4 on v3

--- a/solution.py
+++ b/solution.py
@@ -17,16 +17,24 @@
 def kernel(
     n,
     cap,
-    wanted,
+    batch_ids,
+    cond_ids,
+    home,
     noise,
     latent_any,
     diag,
     cond,
     obs,
     out,
+    found,
+    wanted,
+    asked,
     every,
     tables,
     scalars,
+    slots,
+    flipped,
+    hits,
     latent,
     outgoing,
     fetched_left,
@@ -84,15 +92,46 @@
         )
 
     pl.semaphore_signal(barrier, inc=1, device_id=partner, device_id_type=MESH)
+
+    @pl.loop(0, rows, unroll=8)
+    def _(r):
+        found[0, 4 * r] = home[batch_ids[r]]
+        for k in range(3):
+            found[0, 4 * r + k + 1] = home[cond_ids[k, r]]
+
+    to_vector = pltpu.make_async_copy(found, wanted, load_sem.at[3])
+    to_vector.start()
+    to_vector.wait()
+
+    lane = lax.broadcasted_iota(jnp.int32, (n, want), 1)
+    owner = lax.broadcasted_iota(jnp.int32, (n, want), 0)
+    slot = jnp.broadcast_to(wanted[...], (n, want)) - owner * per_owner
+    mine = (slot >= 0) & (slot < per_owner)
+    rank = jnp.where(mine, 1, 0)
+    shift = 1
+    while shift < want:
+        rank = rank + jnp.where(lane >= shift, pltpu.roll(rank, shift, 1), 0)
+        shift *= 2
+    rank = jnp.where(mine, rank - 1, -1)
+
+    def table(value):
+        filled = jnp.zeros((n, want), jnp.int32)
+        for c in range(cap):
+            entry = jnp.sum(jnp.where(rank == c, value, 0), axis=1, keepdims=True)
+            filled = jnp.where(lane == c, entry, filled)
+        return filled
+
+    asked[...] = (table(slot + 1) - 1).reshape(n, 1, want)
     pl.semaphore_wait(barrier, n)
 
     def id_copy(o):
+        dst = peer(o)
         return pltpu.make_async_remote_copy(
-            src_ref=wanted,
+            src_ref=asked.at[dst],
             dst_ref=every.at[me],
             send_sem=id_send.at[o],
             recv_sem=id_recv.at[o],
-            device_id=(peer(o), core),
+            device_id=(dst, core),
             device_id_type=MESH,
         )
 
@@ -100,53 +139,31 @@
     def _(o):
         id_copy(o).start()
 
-    every[me] = wanted[...]
-    lane = lax.broadcasted_iota(jnp.int32, (n, want), 1)
-    owner = lax.broadcasted_iota(jnp.int32, (n, want), 0)
-
-    def ranks(mask):
-        count = jnp.where(mask, 1, 0)
-        shift = 1
-        while shift < want:
-            count = count + jnp.where(lane >= shift, pltpu.roll(count, shift, 1), 0)
-            shift *= 2
-        return count - 1
-
-    def table(mask, rank, value):
-        rank = jnp.where(mask, rank, -1)
-        filled = jnp.zeros((n, want), jnp.int32)
-        for c in range(cap):
-            found = jnp.sum(jnp.where(rank == c, value, 0), axis=1, keepdims=True)
-            filled = jnp.where(lane == c, found, filled)
-        return filled
-
-    mine = jnp.broadcast_to(wanted[...], (n, want)) - owner * per_owner
-    mine = (mine >= 0) & (mine < per_owner)
-    rank = ranks(mine)
-    tables[pl.ds(n, n)] = table(mine, rank, lane)
+    every[me] = asked[me]
+    tables[pl.ds(0, n)] = table(lane)
     spot = jnp.sum(jnp.where(mine, owner * cap + rank, 0), axis=0, keepdims=True)
-    tables[pl.ds(2 * n, 8)] = jnp.broadcast_to(spot, (8, want))
-
-    @pl.loop(1, n)
-    def _(o):
-        id_copy(o).wait_recv()
-
-    slot = every[...].reshape(n, want) - me * per_owner
-    mine = (slot >= 0) & (slot < per_owner)
-    tables[pl.ds(0, n)] = table(mine, ranks(mine), slot + 1) - 1
+    tables[pl.ds(n, 8)] = jnp.broadcast_to(spot, (8, want))
     to_scalars = pltpu.make_async_copy(tables, scalars, load_sem.at[3])
     to_scalars.start()
+
+    @pl.loop(1, n)
+    def _(o):
+        id_copy(o).wait_recv()
+
+    to_slots = pltpu.make_async_copy(every, slots, load_sem.at[4])
+    to_slots.start()
     load_latent.wait()
+    to_slots.wait()
     to_scalars.wait()
 
     def slot_of(owner, c):
-        return jnp.maximum(scalars[owner, c], 0)
+        return jnp.maximum(slots[owner, 0, c], 0)
 
     def term_of(owner, c):
-        return scalars[n + owner, c]
+        return scalars[owner, c]
 
     def panel_of(w):
-        return scalars[2 * n, w]
+        return scalars[n, w]
 
     def latent_copy(h, o):
         dst = peer(o)
@@ -176,32 +193,43 @@
             fetched[h][me * cap + c] = latent[slot_of(me, c), :, part]
 
     outbox[...] = jnp.zeros_like(outbox)
+    pad = outbox.shape[1]
     load_diag.wait()
+    load_cond.wait()
     keep = lax.broadcasted_iota(jnp.int32, (width, width), 0) >= lax.broadcasted_iota(
         jnp.int32, (width, width), 1
     )
-
-    @pl.loop(0, rows)
-    def _(r):
-        lower[r] = jnp.where(keep, lower[r], jnp.zeros((width, width), bf16))
+    share = -(-rows // (n - 1))
 
     @pl.loop(0, n - 1)
     def _(k):
+        for i in range(share):
+            r = k * share + i
+
+            @pl.when(r < rows)
+            def _():
+                lower[r] = jnp.where(keep, lower[r], jnp.zeros((width, width), bf16))
+                flipped[r, pl.ds(0, half)] = lower[r, :, half:].T
+                for j in range(3):
+                    flipped[r, pl.ds((j + 1) * half, half)] = near[r, j, :, half:].T
+
         latent_copy(0, turn(k)).wait_send()
         pack(1, turn(k))
 
-    load_cond.wait()
-
-    def product(h, r):
-        part = slice(h * half, (h + 1) * half)
-        panels = [fetched[h][panel_of(4 * r + k)] for k in range(4)]
-        blocks = [lower[r, :, part]] + [near[r, k, :, part] for k in range(3)]
-        return lax.dot_general(
-            jnp.concatenate(panels, axis=1),
-            jnp.concatenate(blocks, axis=1),
-            NT,
-            preferred_element_type=f32,
-        )
+    position = lax.broadcasted_iota(jnp.int32, (per_owner, want), 0)
+    spread = lax.broadcasted_iota(jnp.int32, (1, want), 1)
+
+    @pl.loop(0, n)
+    def _(source):
+        row = every[source]
+        row = jnp.where(spread < pad, row, -1)
+        row = jnp.maximum(row, jnp.where(spread >= pad, pltpu.roll(row, pad, 1), -1))
+        row = jnp.maximum(row, jnp.where(spread >= 2 * pad, pltpu.roll(row, pad, 1), -1))
+        row = jnp.where(spread < 3 * pad, row, -1)
+        hits[source] = jnp.where(position == row, 1.0, 0.0).astype(bf16)
+
+    def panels(h, r):
+        return jnp.concatenate([fetched[h][panel_of(4 * r + k)] for k in range(4)], axis=1)
 
     @pl.loop(1, n)
     def _(o):
@@ -209,7 +237,10 @@
 
     @pl.loop(0, rows, unroll=4)
     def _(r):
-        partial[r] = product(0, r)
+        blocks = [lower[r, :, :half]] + [near[r, k, :, :half] for k in range(3)]
+        partial[r] = lax.dot_general(
+            panels(0, r), jnp.concatenate(blocks, axis=1), NT, preferred_element_type=f32
+        )
 
     @pl.loop(1, n)
     def _(o):
@@ -234,7 +265,7 @@
         @pl.loop(0, group, unroll=4)
         def _(i):
             r = g * group + i
-            white = partial[r] + product(1, r)
+            white = partial[r] + jnp.dot(panels(1, r), flipped[r], preferred_element_type=f32)
             scored = (freedom + 1.0) * white / (freedom + white * white)
             low = scored.astype(bf16).astype(f32)
             sums[g, pl.ds(i, 1)] = jnp.sum(low, axis=0, keepdims=True)
@@ -287,19 +318,14 @@
     for c in range(cap):
         outbox[me, pl.ds(c, 1)] = terms[pl.ds(term_of(me, c), 1)]
     inbox[me] = outbox[me]
-    pad = outbox.shape[1]
-    place = lax.broadcasted_iota(jnp.int32, (per_owner, want), 0)
 
     def collect(source):
-        hits = jnp.where(place == tables[pl.ds(source, 1)], 1.0, 0.0).astype(bf16)[:, :pad]
         arrived = inbox[source]
         first = arrived.astype(bf16)
         rest = arrived - first.astype(f32)
-        second = rest.astype(bf16)
-        third = (rest - second.astype(f32)).astype(bf16)
-        total = jnp.dot(hits, first, preferred_element_type=f32)
-        total = total + jnp.dot(hits, second, preferred_element_type=f32)
-        return total + jnp.dot(hits, third, preferred_element_type=f32)
+        second = rest.astype(bf16).astype(f32)
+        parts = jnp.concatenate([first.astype(f32), second, rest - second], axis=0).astype(bf16)
+        return jnp.dot(hits[source][:, : 3 * pad], parts, preferred_element_type=f32)
 
     out[...] = collect(me)
 
@@ -325,21 +351,24 @@
     want = 4 * rows
     cap = max(2, 10 * rows // n)
     pad = -(-cap // 8) * 8
-    block_ids = jnp.concatenate([batch_ids[:, None], cond_ids], axis=1).reshape(-1)
-    wanted = home[block_ids].reshape(1, want)
-
     smem = pl.BlockSpec(memory_space=pltpu.SMEM)
     vmem = pl.BlockSpec(memory_space=pltpu.VMEM)
     anywhere = pl.BlockSpec(memory_space=pl.ANY)
     return pl.pallas_call(
         functools.partial(kernel, n, cap),
         out_shape=jax.ShapeDtypeStruct((per_owner, width // 2), f32),
-        in_specs=[vmem, smem, anywhere, anywhere, anywhere, vmem],
+        in_specs=[smem, smem, smem, smem, anywhere, anywhere, anywhere, vmem],
         out_specs=vmem,
         scratch_shapes=[
+            pltpu.SMEM((1, want), jnp.int32),
+            pltpu.VMEM((1, want), jnp.int32),
             pltpu.VMEM((n, 1, want), jnp.int32),
-            pltpu.VMEM((2 * n + 8, want), jnp.int32),
-            pltpu.SMEM((2 * n + 8, want), jnp.int32),
+            pltpu.VMEM((n, 1, want), jnp.int32),
+            pltpu.VMEM((n + 8, want), jnp.int32),
+            pltpu.SMEM((n + 8, want), jnp.int32),
+            pltpu.SMEM((n, 1, want), jnp.int32),
+            pltpu.VMEM((rows, 2 * width, width), bf16),
+            pltpu.VMEM((n, per_owner, want), bf16),
             pltpu.VMEM(latent.shape, bf16),
             pltpu.VMEM((2, n, cap, draws, width // 2), bf16),
             pltpu.VMEM((n * cap, draws, width // 2), bf16),
@@ -352,7 +381,7 @@
             pltpu.VMEM((want, width // 2), f32),
             pltpu.VMEM((n, pad, width // 2), f32),
             pltpu.VMEM((n, pad, width // 2), f32),
-            pltpu.SemaphoreType.DMA((4,)),
+            pltpu.SemaphoreType.DMA((5,)),
             pltpu.SemaphoreType.DMA((n,)),
             pltpu.SemaphoreType.DMA((n,)),
             pltpu.SemaphoreType.DMA((2 * n,)),
@@ -364,7 +393,7 @@
         compiler_params=pltpu.CompilerParams(
             collective_id=0, has_side_effects=True, vmem_limit_bytes=56 * 1024 * 1024
         ),
-    )(wanted, noise_prec.reshape(1), latent, diag_factor, cond_factor, obs)
+    )(batch_ids, cond_ids.T, home, noise_prec.reshape(1), latent, diag_factor, cond_factor, obs)
 
 
 def solution(mesh):

time: 89.6 us -> 85.5 us (0.954)
  local copies, waits for them, and re-layouts: 3.44 us -> 1.57 us
  Pallas kernels: 84.5 us -> 83.1 us
    gather x1 -> x0, local copies, waits for them, and re-layouts: 1.67 us -> none  [body(): wanted = home[block_ids].reshape(1, want)]
    pallas_call x1, Pallas kernels: 84.5 us -> 83.1 us  [body(): pl.pallas_call(functools.partial(kernel, n, cap), out_shape=jax.ShapeDtyp...]
where the time goes in v4:
time: 85.5 us; the launch traced here: 85.3 us
  Pallas kernels  83.1 us (97%)
  local copies, waits for them, and re-layouts  1.57 us (2%)
    pallas_call x1, Pallas kernels, body(): pl.pallas_call(functools.partial(kernel, n, cap), out_shape=jax.ShapeDtyp...  83.1 us

profile of v4, /device:TPU:0, one launch (start us, length us, event | category | flops | bytes accessed | tf_op | source)
XLA Modules:
  0.0 85.3 jit_solution(12729622552058069973)
XLA Ops:
  0.7 83.1 %shard_map.82 = f32[256,128]{1,0:T(8,128)} custom-call(s32[32]{0:T(128)} %batch_ids.1, s32[3,32]{1,0:T(4,128)} %bitcast.3, s32[4096]{0:T(1024)} %home.1, f32[1]{0:T(128)} %bitcast.2.noise, bf16[256,16,256]{2,1,0:T(8,128)(2,1)} %latent_any.1, bf16[32,256,256]{2,1,0:T(8,128)(2,1)} %diag.1, bf16[32,3,256,256]{3,2,1,0:T(8,128)(2,1)} %cond.1, f32[32,256]{1,0:T(8,128)} %obs.1), custom_call_target="tpu_custom_call" | custom-call | tf_op jit(solution)/shard_map/pallas_call | solution.py:357
  83.8 1.6 %copy.11 = f32[256,128]{1,0:T(8,128)} copy(f32[256,128]{1,0:T(8,128)} %shard_map.82) | data formatting | bytes 262144

commit v5 on v4

--- a/solution.py
+++ b/solution.py
@@ -209,12 +209,15 @@
             @pl.when(r < rows)
             def _():
                 lower[r] = jnp.where(keep, lower[r], jnp.zeros((width, width), bf16))
-                flipped[r, pl.ds(0, half)] = lower[r, :, half:].T
-                for j in range(3):
-                    flipped[r, pl.ds((j + 1) * half, half)] = near[r, j, :, half:].T
 
         latent_copy(0, turn(k)).wait_send()
         pack(1, turn(k))
+
+    @pl.loop(0, rows)
+    def _(r):
+        flipped[r, pl.ds(0, half)] = lower[r, :, half:].T
+        for j in range(3):
+            flipped[r, pl.ds((j + 1) * half, half)] = near[r, j, :, half:].T
 
     position = lax.broadcasted_iota(jnp.int32, (per_owner, want), 0)
     spread = lax.broadcasted_iota(jnp.int32, (1, want), 1)
@@ -262,7 +265,7 @@
 
     for g in range(2):
 
-        @pl.loop(0, group, unroll=4)
+        @pl.loop(0, group, unroll=8)
         def _(i):
             r = g * group + i
             white = partial[r] + jnp.dot(panels(1, r), flipped[r], preferred_element_type=f32)
@@ -279,22 +282,22 @@
         swap(g).wait_recv()
         sums_in[g] = sums_in[g] + sums[g]
 
-        @pl.loop(0, group, unroll=4)
+        @pl.loop(0, group, unroll=8)
         def _(i):
             r = g * group + i
             total = jnp.broadcast_to(sums_in[g, pl.ds(i, 1)], (16, width))
             high = total.astype(bf16).astype(f32)
             parts = jnp.where(place == 0, high, jnp.where(place == 1, total - high, 0.0)).astype(bf16)
-            back = jnp.dot(parts, lower[r, :, column], preferred_element_type=f32)
-            back = jnp.sum(back, axis=0, keepdims=True)
+            blocks = [lower[r, :, column]] + [near[r, k, :, column] for k in range(3)]
+            back = jnp.dot(parts, jnp.concatenate(blocks, axis=1), preferred_element_type=f32)
+            back = (back[0:1] + back[1:2]) * inverse_draws
             own = sums_in[g, pl.ds(group + i, 1)]
             likely = noise[0] * (2 * draws * obs[pl.ds(r, 1)] - own)
             likely = jnp.where(core == 0, likely[:, :half], likely[:, half:])
-            terms[pl.ds(4 * r, 1)] = (likely - back) * inverse_draws
+            terms[pl.ds(4 * r, 1)] = likely * inverse_draws - back[:, :half]
             for k in range(3):
-                back = jnp.dot(parts, near[r, k, :, column], preferred_element_type=f32)
-                back = jnp.sum(back, axis=0, keepdims=True)
-                terms[pl.ds(4 * r + k + 1, 1)] = -back * inverse_draws
+                part = slice((k + 1) * half, (k + 2) * half)
+                terms[pl.ds(4 * r + k + 1, 1)] = -back[:, part]
 
     def term_copy(o):
         dst = peer(o)
@@ -327,12 +330,13 @@
         parts = jnp.concatenate([first.astype(f32), second, rest - second], axis=0).astype(bf16)
         return jnp.dot(hits[source][:, : 3 * pad], parts, preferred_element_type=f32)
 
-    out[...] = collect(me)
+    out[0] = collect(me)
+    out[1] = jnp.zeros_like(out[1])
 
     @pl.loop(1, n)
     def _(o):
         term_copy(o).wait_recv()
-        out[...] += collect(peer(o))
+        out[lax.rem(o, 2)] += collect(peer(o))
 
     @pl.loop(1, n)
     def _(o):
@@ -354,9 +358,9 @@
     smem = pl.BlockSpec(memory_space=pltpu.SMEM)
     vmem = pl.BlockSpec(memory_space=pltpu.VMEM)
     anywhere = pl.BlockSpec(memory_space=pl.ANY)
-    return pl.pallas_call(
+    partial_sums = pl.pallas_call(
         functools.partial(kernel, n, cap),
-        out_shape=jax.ShapeDtypeStruct((per_owner, width // 2), f32),
+        out_shape=jax.ShapeDtypeStruct((2, per_owner, width // 2), f32),
         in_specs=[smem, smem, smem, smem, anywhere, anywhere, anywhere, vmem],
         out_specs=vmem,
         scratch_shapes=[
@@ -394,6 +398,7 @@
             collective_id=0, has_side_effects=True, vmem_limit_bytes=56 * 1024 * 1024
         ),
     )(batch_ids, cond_ids.T, home, noise_prec.reshape(1), latent, diag_factor, cond_factor, obs)
+    return partial_sums[0] + partial_sums[1]
 
 
 def solution(mesh):

time: 85.5 us -> 84.8 us (level)
  other arithmetic: 0 us -> 1.64 us
  local copies, waits for them, and re-layouts: 1.57 us -> 0 us
    add x0 -> x1, other arithmetic: none -> 1.64 us  [body(): return partial_sums[0] + partial_sums[1]]
    unnamed x1 -> x0, local copies, waits for them, and re-layouts: 1.57 us -> none
where the time goes in v5:
time: 84.8 us; the launch traced here: 84.6 us
  Pallas kernels  82.3 us (97%)
  other arithmetic  1.64 us (2%)
    pallas_call x1, Pallas kernels, body(): pl.pallas_call(functools.partial(kernel, n, cap), out_shape=jax.ShapeDtyp...  82.3 us

profile of v5, /device:TPU:0, one launch (start us, length us, event | category | flops | bytes accessed | tf_op | source)
XLA Modules:
  0.0 84.6 jit_solution(6158156115360713516)
XLA Ops:
  0.7 82.3 %shard_map.82 = f32[2,256,128]{2,1,0:T(8,128)} custom-call(s32[32]{0:T(128)} %batch_ids.1, s32[3,32]{1,0:T(4,128)} %bitcast.5, s32[4096]{0:T(1024)} %home.1, f32[1]{0:T(128)} %bitcast.4.noise, bf16[256,16,256]{2,1,0:T(8,128)(2,1)} %latent_any.1, bf16[32,256,256]{2,1,0:T(8,128)(2,1)} %diag.1, bf16[32,3,256,256]{3,2,1,0:T(8,128)(2,1)} %cond.1, f32[32,256]{1,0:T(8,128)} %obs.1), custom_call_target="tpu_custom_call" | custom-call | tf_op jit(solution)/shard_map/pallas_call | solution.py:361
  83.0 1.6 %add_bitcast_fusion = f32[256,128]{1,0:T(8,128)} fusion(f32[2,256,128]{2,1,0:T(8,128)} %shard_map.82), kind=kLoop, calls=%fused_computation | loop fusion | flops 32768 | bytes 393216 | tf_op jit(solution)/shard_map/add | solution.py:401

commit v6 on v5

--- a/solution.py
+++ b/solution.py
@@ -80,8 +80,6 @@
     load_diag = pltpu.make_async_copy(diag, lower, load_sem.at[0])
     load_cond = pltpu.make_async_copy(cond, near, load_sem.at[1])
     load_latent.start()
-    load_diag.start()
-    load_cond.start()
 
     barrier = pltpu.get_barrier_semaphore()
 
@@ -181,11 +179,29 @@
         part = slice(h * half, (h + 1) * half)
         for c in range(cap):
             outgoing[h, dst, c] = latent[slot_of(dst, c), :, part]
-        latent_copy(h, o).start()
 
     @pl.loop(0, n - 1)
     def _(k):
         pack(0, turn(k))
+        latent_copy(0, turn(k)).start()
+
+    lead = n // 4
+
+    @pl.loop(0, lead)
+    def _(k):
+        pack(1, n // 2 + k)
+        latent_copy(1, n // 2 + k).start()
+
+    load_diag.start()
+    load_cond.start()
+
+    @pl.loop(0, n - 1)
+    def _(k):
+        o = turn(k)
+
+        @pl.when((o < n // 2) | (o >= n // 2 + lead))
+        def _():
+            pack(1, o)
 
     for h in range(2):
         part = slice(h * half, (h + 1) * half)
@@ -210,8 +226,12 @@
             def _():
                 lower[r] = jnp.where(keep, lower[r], jnp.zeros((width, width), bf16))
 
-        latent_copy(0, turn(k)).wait_send()
-        pack(1, turn(k))
+        o = turn(k)
+        latent_copy(0, o).wait_send()
+
+        @pl.when((o < n // 2) | (o >= n // 2 + lead))
+        def _():
+            latent_copy(1, o).start()
 
     @pl.loop(0, rows)
     def _(r):

time: 84.8 us -> 84.8 us (level)
  no operation moved by 1% of the time
where the time goes in v6:
time: 84.8 us; the launch traced here: 84.6 us
  Pallas kernels  82.3 us (97%)
  other arithmetic  1.64 us (2%)
    pallas_call x1, Pallas kernels, body(): pl.pallas_call(functools.partial(kernel, n, cap), out_shape=jax.ShapeDtyp...  82.3 us

profile of v6, /device:TPU:0, one launch (start us, length us, event | category | flops | bytes accessed | tf_op | source)
XLA Modules:
  0.0 84.6 jit_solution(15865504160896405424)
XLA Ops:
  0.7 82.3 %shard_map.82 = f32[2,256,128]{2,1,0:T(8,128)} custom-call(s32[32]{0:T(128)} %batch_ids.1, s32[3,32]{1,0:T(4,128)} %bitcast.5, s32[4096]{0:T(1024)} %home.1, f32[1]{0:T(128)} %bitcast.4.noise, bf16[256,16,256]{2,1,0:T(8,128)(2,1)} %latent_any.1, bf16[32,256,256]{2,1,0:T(8,128)(2,1)} %diag.1, bf16[32,3,256,256]{3,2,1,0:T(8,128)(2,1)} %cond.1, f32[32,256]{1,0:T(8,128)} %obs.1), custom_call_target="tpu_custom_call" | custom-call | tf_op jit(solution)/shard_map/pallas_call | solution.py:381
  83.0 1.6 %add_bitcast_fusion = f32[256,128]{1,0:T(8,128)} fusion(f32[2,256,128]{2,1,0:T(8,128)} %shard_map.82), kind=kLoop, calls=%fused_computation | loop fusion | flops 32768 | bytes 393216 | tf_op jit(solution)/shard_map/add | solution.py:421

commit v7 on v6

--- a/solution.py
+++ b/solution.py
@@ -26,8 +26,6 @@
     cond,
     obs,
     out,
-    found,
-    wanted,
     asked,
     every,
     tables,
@@ -91,19 +89,18 @@
 
     pl.semaphore_signal(barrier, inc=1, device_id=partner, device_id_type=MESH)
 
-    @pl.loop(0, rows, unroll=8)
-    def _(r):
-        found[0, 4 * r] = home[batch_ids[r]]
+    entry_lane = lax.broadcasted_iota(jnp.int32, (8, want), 1)
+
+    def look_up(r, known):
+        known = jnp.where(entry_lane == 4 * r, home[batch_ids[r]], known)
         for k in range(3):
-            found[0, 4 * r + k + 1] = home[cond_ids[k, r]]
-
-    to_vector = pltpu.make_async_copy(found, wanted, load_sem.at[3])
-    to_vector.start()
-    to_vector.wait()
-
+            known = jnp.where(entry_lane == 4 * r + k + 1, home[cond_ids[k, r]], known)
+        return known
+
+    wanted = lax.fori_loop(0, rows, look_up, jnp.zeros((8, want), jnp.int32), unroll=8)
     lane = lax.broadcasted_iota(jnp.int32, (n, want), 1)
     owner = lax.broadcasted_iota(jnp.int32, (n, want), 0)
-    slot = jnp.broadcast_to(wanted[...], (n, want)) - owner * per_owner
+    slot = jnp.broadcast_to(wanted[0:1], (n, want)) - owner * per_owner
     mine = (slot >= 0) & (slot < per_owner)
     rank = jnp.where(mine, 1, 0)
     shift = 1
@@ -208,8 +205,7 @@
         for c in range(cap):
             fetched[h][me * cap + c] = latent[slot_of(me, c), :, part]
 
-    outbox[...] = jnp.zeros_like(outbox)
-    pad = outbox.shape[1]
+    pad = -(-cap // 8) * 8
     load_diag.wait()
     load_cond.wait()
     keep = lax.broadcasted_iota(jnp.int32, (width, width), 0) >= lax.broadcasted_iota(
@@ -343,7 +339,8 @@
     inbox[me] = outbox[me]
 
     def collect(source):
-        arrived = inbox[source]
+        blank = jnp.zeros((pad - cap, half), f32)
+        arrived = jnp.concatenate([inbox[source], blank], axis=0) if pad > cap else inbox[source]
         first = arrived.astype(bf16)
         rest = arrived - first.astype(f32)
         second = rest.astype(bf16).astype(f32)
@@ -374,7 +371,6 @@
     rows = batch_ids.shape[0]
     want = 4 * rows
     cap = max(2, 10 * rows // n)
-    pad = -(-cap // 8) * 8
     smem = pl.BlockSpec(memory_space=pltpu.SMEM)
     vmem = pl.BlockSpec(memory_space=pltpu.VMEM)
     anywhere = pl.BlockSpec(memory_space=pl.ANY)
@@ -384,8 +380,6 @@
         in_specs=[smem, smem, smem, smem, anywhere, anywhere, anywhere, vmem],
         out_specs=vmem,
         scratch_shapes=[
-            pltpu.SMEM((1, want), jnp.int32),
-            pltpu.VMEM((1, want), jnp.int32),
             pltpu.VMEM((n, 1, want), jnp.int32),
             pltpu.VMEM((n, 1, want), jnp.int32),
             pltpu.VMEM((n + 8, want), jnp.int32),
@@ -403,8 +397,8 @@
             pltpu.VMEM((2, rows, width), f32),
             pltpu.VMEM((2, rows, width), f32),
             pltpu.VMEM((want, width // 2), f32),
-            pltpu.VMEM((n, pad, width // 2), f32),
-            pltpu.VMEM((n, pad, width // 2), f32),
+            pltpu.VMEM((n, cap, width // 2), f32),
+            pltpu.VMEM((n, cap, width // 2), f32),
             pltpu.SemaphoreType.DMA((5,)),
             pltpu.SemaphoreType.DMA((n,)),
             pltpu.SemaphoreType.DMA((n,)),

time: 84.8 us -> 84.3 us (level)
  no operation moved by 1% of the time
where the time goes in v7:
time: 84.3 us; the launch traced here: 84 us
  Pallas kernels  81.7 us (97%)
  other arithmetic  1.64 us (2%)
    pallas_call x1, Pallas kernels, body(): pl.pallas_call(functools.partial(kernel, n, cap), out_shape=jax.ShapeDtyp...  81.7 us

profile of v7, /device:TPU:0, one launch (start us, length us, event | category | flops | bytes accessed | tf_op | source)
XLA Modules:
  0.0 84.0 jit_solution(9981668322189070849)
XLA Ops:
  0.7 81.7 %shard_map.82 = f32[2,256,128]{2,1,0:T(8,128)} custom-call(s32[32]{0:T(128)} %batch_ids.1, s32[3,32]{1,0:T(4,128)} %bitcast.5, s32[4096]{0:T(1024)} %home.1, f32[1]{0:T(128)} %bitcast.4.noise, bf16[256,16,256]{2,1,0:T(8,128)(2,1)} %latent_any.1, bf16[32,256,256]{2,1,0:T(8,128)(2,1)} %diag.1, bf16[32,3,256,256]{3,2,1,0:T(8,128)(2,1)} %cond.1, f32[32,256]{1,0:T(8,128)} %obs.1), custom_call_target="tpu_custom_call" | custom-call | tf_op jit(solution)/shard_map/pallas_call | solution.py:377
  82.4 1.6 %add_bitcast_fusion = f32[256,128]{1,0:T(8,128)} fusion(f32[2,256,128]{2,1,0:T(8,128)} %shard_map.82), kind=kLoop, calls=%fused_computation | loop fusion | flops 32768 | bytes 393216 | tf_op jit(solution)/shard_map/add | solution.py:415
